TPU v7x, 32 devices: a whole 2x2x4 slice. The times are simulated.
32 devices in a mesh: mode: 4 (over y, core), blk: 8 (over z, x).
Axes of the slice: x: 2, y: 2, z: 4, core: 2. Of those that a mesh axis runs over, the one named last changes fastest.
Arguments:
- divergence: float32 [8, 32, 128, 1024], P('blk', None, 'mode')
- neighbours: int32 [8, 2], P('blk'), may hold values from -1 to 7, as said below
- levels: int32 [8], P('blk'), may hold values from 0 to 2
- sweeps: int32 [3], replicated, may hold values from 1 to 2, as said below
Outputs:
- pressure: float32 [8, 32, 128, 1024], P('blk', None, 'mode')
Inputs may be any that keep to these rules, and one draw needn't show every extreme that they name: `neighbours`: row b holds the slots of the columns west (entry 0) and east (entry 1) of the column in slot b along x, -1 beyond the two ends of the 8 columns. The lists are mutual, every slot is named, and every neighbour's slot lies within 3 of b, exactly 3 away for some. Some level has 2 sweeps.
All inputs are finite; a program needn't handle non-finite values.
Results may differ from a plain program's by a relative error of at most 0.0003.
Values sent between devices are 32-bit elements; how exact they have to be, the bound alone decides.
A program may use at most 128 MiB of HBM per device.

v0:
```python
import functools

import jax
import jax.numpy as jnp
import ml_dtypes
import numpy as np
from jax import lax
from jax.experimental import pallas as pl
from jax.experimental.pallas import tpu as pltpu
from jax.sharding import PartitionSpec as P

SWEEPS = 2
CITERS = 8
DAMPING = 0.8
HIGH = lax.Precision.HIGH
HIGHEST = lax.Precision.HIGHEST


def sine_table(extent):
    ordinal = np.arange(1, extent + 1)
    phases = np.outer(ordinal, ordinal) % (2 * (extent + 1))
    matrix = np.sqrt(2.0 / (extent + 1)) * np.sin(phases * (np.pi / (extent + 1)))
    eigen = 2.0 - 2.0 * np.cos(ordinal * (np.pi / (extent + 1)))
    return matrix, eigen


def fourier_table(length):
    half = length // 2
    ids = np.arange(length)
    wave = np.where(ids <= half, ids, ids - half)
    angles = (np.outer(wave, ids) % length) * (2.0 * np.pi / length)
    fourier = np.where((ids <= half)[:, None], np.cos(angles), np.sin(angles))
    weights = np.where((ids == 0) | (ids == half), 1.0, 2.0) / length
    shift = 2.0 - 2.0 * np.cos(wave * (2.0 * np.pi / length))
    return fourier, weights, shift


def f32(array):
    return jnp.asarray(np.asarray(array, np.float32))


def exchange_kernel(columns, n, src, dst, send_sem, recv_sem, own_sem):
    me = lax.axis_index("mode") * columns + lax.axis_index("blk")

    def place(slot):
        return {"mode": slot // columns, "blk": lax.rem(slot, columns)}

    def send(step):
        peer = lax.rem(me + step, n)
        return pltpu.make_async_remote_copy(
            src_ref=src.at[peer],
            dst_ref=dst.at[me],
            send_sem=send_sem.at[step],
            recv_sem=recv_sem.at[step],
            device_id=place(peer),
            device_id_type=pl.DeviceIdType.MESH,
        )

    barrier = pltpu.get_barrier_semaphore()

    @pl.loop(1, n)
    def _(step):
        pl.semaphore_signal(
            barrier,
            inc=1,
            device_id=place(lax.rem(me + step, n)),
            device_id_type=pl.DeviceIdType.MESH,
        )

    own = pltpu.make_async_copy(src.at[me], dst.at[me], own_sem)
    own.start()
    pl.semaphore_wait(barrier, n - 1)

    @pl.loop(1, n)
    def _(step):
        send(step).start()

    own.wait()

    @pl.loop(1, n)
    def _(step):
        send(step).wait()


def exchange(values, number):
    columns = lax.axis_size("blk")
    n = lax.axis_size("mode") * columns
    return pl.pallas_call(
        functools.partial(exchange_kernel, columns, n),
        out_shape=jax.ShapeDtypeStruct(values.shape, values.dtype),
        in_specs=[pl.BlockSpec(memory_space=pltpu.VMEM)],
        out_specs=pl.BlockSpec(memory_space=pltpu.VMEM),
        scratch_shapes=[
            pltpu.SemaphoreType.DMA((n,)),
            pltpu.SemaphoreType.DMA((n,)),
            pltpu.SemaphoreType.DMA,
        ],
        compiler_params=pltpu.CompilerParams(collective_id=number, has_side_effects=True),
        name=f"exchange_{number}",
    )(values)


def pack(rows, blocks):
    share = rows.shape[1] // blocks
    rows = rows.reshape(rows.shape[0], blocks, share).transpose(1, 0, 2)
    return rows.reshape(blocks, -1, 128)


def unpack(parcels, share):
    blocks = parcels.shape[0]
    rows = parcels.reshape(blocks, -1, share).transpose(1, 0, 2)
    return rows.reshape(-1, blocks * share)


def split(array):
    high = array.astype(jnp.bfloat16)
    return high, (array - high.astype(jnp.float32)).astype(jnp.bfloat16)


def split_table(array):
    array = np.asarray(array, np.float32)
    high = array.astype(ml_dtypes.bfloat16)
    low = (array - high.astype(np.float32)).astype(ml_dtypes.bfloat16)
    return jnp.asarray(high), jnp.asarray(low)


def dot3(a_high, a_low, b_high, b_low):
    def dot(a, b):
        return jnp.dot(a, b, preferred_element_type=jnp.float32)

    return dot(a_high, b_high) + (dot(a_high, b_low) + dot(a_low, b_high))


def inverse_of(value):
    guess = pl.reciprocal(value, approx=True)
    return guess * (2.0 - value * guess)


def parity_order(bx):
    return list(range(0, bx, 2)) + list(range(1, bx, 2))


def parity_tables(bx, nl):
    sx, _ = sine_table(bx)
    sl, _ = sine_table(nl)
    return [np.kron(sx[: bx // 2, part::2], sl) for part in (0, 1)]


def forward_kernel(bx, nl, lx, s0, x, fh, fl, kh, kl, lam, e0, e1, lane, vhat, rows, ah, al):
    half = bx // 2
    side = half * nl

    @pl.when(pl.program_id(0) == 0)
    def _():
        for c in range(half):
            top, bottom = x[0, c], x[0, bx - 1 - c]
            for part, value in ((0, top + bottom), (1, top - bottom)):
                high, low = split(value)
                ah[pl.ds((part * half + c) * nl, nl), :] = high
                al[pl.ds((part * half + c) * nl, nl), :] = low

    base = lam[...] + lane[0:1, :]
    scale = lane[1:2, :]
    sums = []
    for part in range(2):
        own = pl.ds(part * side, side)
        spectrum = dot3(ah[own, :], al[own, :], fh[...], fl[...])
        high, low = split(spectrum)
        ghat = dot3(kh[part], kl[part], high, low)
        total = None
        for c in range(half):
            i = part * half + c
            value = ghat[c * nl : (c + 1) * nl] * (scale * inverse_of(base + lx[i]))
            vhat[pl.ds(i * nl, nl), :] = value
            rows[pl.ds(i, 1), :] = jnp.sum(value * e0[...], axis=0, keepdims=True)
            rows[pl.ds(bx + i, 1), :] = jnp.sum(value * e1[...], axis=0, keepdims=True)
            term = value * s0[i]
            total = term if total is None else total + term
        sums.append(total)
    rows[pl.ds(2 * bx, nl), :] = sums[0] + sums[1]
    rows[pl.ds(2 * bx + nl, nl), :] = sums[0] - sums[1]


def inverse_kernel(bx, nl, lx, s0, tile, vhat, rows, fh, fl, kh, kl, lam, e0, e1, lane, out, uh, ul):
    half = bx // 2
    side = half * nl

    @pl.when(pl.program_id(0) == 0)
    def _():
        @pl.loop(0, vhat.shape[1] // tile)
        def _(step):
            q = pl.ds(pl.multiple_of(step * tile, tile), tile)
            base = lam[...] + lane[0:1, q]
            west, east = rows[pl.ds(2 * bx, nl), q], rows[pl.ds(2 * bx + nl, nl), q]
            for part in range(2):
                face = west + east if part == 0 else west - east
                parts = []
                for c in range(half):
                    i = part * half + c
                    load = (
                        face * s0[i] + rows[pl.ds(i, 1), q] * e0[...] + rows[pl.ds(bx + i, 1), q] * e1[...]
                    )
                    parts.append(vhat[pl.ds(i * nl, nl), q] + load * inverse_of(base + lx[i]))
                high, low = split(jnp.concatenate(parts))
                high, low = split(dot3(kh[part], kl[part], high, low))
                uh[pl.ds(part * side, side), q] = high
                ul[pl.ds(part * side, side), q] = low

    even = dot3(uh[pl.ds(0, side), :], ul[pl.ds(0, side), :], fh[...], fl[...])
    odd = dot3(uh[pl.ds(side, side), :], ul[pl.ds(side, side), :], fh[...], fl[...])
    for c in range(half):
        here = slice(c * nl, (c + 1) * nl)
        out[0, c] = even[here] + odd[here]
        out[0, bx - 1 - c] = even[here] - odd[here]


def local_tables(bx, nl):
    sx, lx = sine_table(bx)
    sl, ll = sine_table(nl)
    order = parity_order(bx)
    return (
        tuple(float(lx[i]) for i in order),
        tuple(float(sx[0, i]) for i in order),
        f32(ll[:, None]),
        f32(sl[0][:, None]),
        f32(sl[-1][:, None]),
    )


def whole_block(array):
    return pl.BlockSpec(array.shape, lambda t: (0,) * array.ndim)


LIMIT = 56 * 1024 * 1024


def forward(divergence, fourier, lane):
    _, bx, nl, ny = divergence.shape
    tile = min(256, ny)
    lx, s0, lam, e0, e1 = local_tables(bx, nl)
    even, odd = parity_tables(bx, nl)
    kh, kl = split_table(np.stack([even.T, odd.T]))
    fh, fl = split_table(fourier.T)
    across = pl.BlockSpec((ny, tile), lambda t: (0, t))
    cells = bx * nl
    count = 2 * bx + 2 * nl
    return pl.pallas_call(
        functools.partial(forward_kernel, bx, nl, lx, s0),
        grid=(ny // tile,),
        out_shape=[
            jax.ShapeDtypeStruct((cells, ny), jnp.float32),
            jax.ShapeDtypeStruct((count, ny), jnp.float32),
        ],
        in_specs=[whole_block(divergence), across, across]
        + [whole_block(a) for a in (kh, kl, lam, e0, e1)]
        + [pl.BlockSpec((8, tile), lambda t: (0, t))],
        out_specs=[
            pl.BlockSpec((cells, tile), lambda t: (0, t)),
            pl.BlockSpec((count, tile), lambda t: (0, t)),
        ],
        scratch_shapes=[pltpu.VMEM((cells, ny), jnp.bfloat16)] * 2,
        compiler_params=pltpu.CompilerParams(vmem_limit_bytes=LIMIT),
        name="forward",
    )(divergence, fh, fl, kh, kl, lam, e0, e1, lane)


def inverse(vhat, rows, weighted, lane, shape):
    _, bx, nl, ny = shape
    tile = min(256, ny)
    lx, s0, lam, e0, e1 = local_tables(bx, nl)
    even, odd = parity_tables(bx, nl)
    kh, kl = split_table(np.stack([even, odd]))
    fh, fl = split_table(weighted)
    across = pl.BlockSpec((ny, tile), lambda t: (0, t))
    cells = bx * nl
    return pl.pallas_call(
        functools.partial(inverse_kernel, bx, nl, lx, s0, tile),
        grid=(ny // tile,),
        out_shape=jax.ShapeDtypeStruct(shape, jnp.float32),
        in_specs=[whole_block(vhat), whole_block(rows), across, across]
        + [whole_block(a) for a in (kh, kl, lam, e0, e1, lane)],
        out_specs=pl.BlockSpec((1, bx, nl, tile), lambda t: (0, 0, 0, t)),
        scratch_shapes=[pltpu.VMEM((cells, ny), jnp.bfloat16)] * 2,
        compiler_params=pltpu.CompilerParams(vmem_limit_bytes=LIMIT),
        name="inverse",
    )(vhat, rows, fh, fl, kh, kl, lam, e0, e1, lane)


def face_response(mu, extent):
    half = 0.5 * mu
    rho = 1.0 / (1.0 + half + jnp.sqrt(mu + half * half))
    rho2 = rho * rho
    power = jnp.ones_like(rho)
    base, left = rho, extent
    while left:
        if left & 1:
            power = power * base
        base, left = base * base, left >> 1
    scale = 1.0 / (1.0 - power * power * rho2)
    return rho * (1.0 - power * power) * scale, power * (1.0 - rho2) * scale


def vcycle(first_face, last_face, facts, mu, tables, allowed, stiffness, shift, share):
    lanes = first_face.shape[1]
    lane = jnp.arange(lanes, dtype=jnp.int32)
    slot, within = lane // share, lane % share
    same = within[:, None] == within[None, :]
    west_hot = (same & (slot[:, None] == facts[0][None, :])).astype(jnp.float32)
    east_hot = (same & (slot[:, None] == facts[1][None, :])).astype(jnp.float32)
    direct, across = face_response(mu, tables["bx"])
    twice = allowed > 1
    weight = tables["z"][:, None]

    def beside(hot, values):
        return jnp.dot(values, hot, precision=HIGHEST)

    def sweep(west, east):
        return (
            first_face + direct * west + across * east,
            last_face + across * west + direct * east,
        )

    used_w, used_e = beside(west_hot, last_face), beside(east_hot, first_face)
    second = sweep(used_w, used_e)
    first = jnp.where(twice, second[0], first_face)
    last = jnp.where(twice, second[1], last_face)
    west, east = beside(west_hot, last), beside(east_hot, first)
    change = west + east - jnp.where(twice, used_w + used_e, 0.0)
    rhs = jnp.sum(change * weight, axis=0) * stiffness
    diagonal = stiffness * tables["perimeter"] + tables["cells"] * shift
    coupling = stiffness * tables["nz"]
    link = west_hot + east_hot
    correction = DAMPING * rhs / diagonal
    for _ in range(CITERS - 1):
        linked = beside(link, correction[None])[0]
        correction = (
            correction + DAMPING * (rhs - diagonal * correction + coupling * linked) / diagonal
        )
    west = west + beside(west_hot, correction[None]) * weight
    east = east + beside(east_hot, correction[None]) * weight
    first, last = sweep(west, east)
    again_w, again_e = beside(west_hot, last), beside(east_hot, first)
    return jnp.where(twice, again_w, west), jnp.where(twice, again_e, east)


def middle(got, sweeps, k, bx, nl, modes, columns):
    nz = nl * modes
    share = k.shape[0] // (modes * columns)
    me = lax.axis_index("mode") * columns + lax.axis_index("blk")
    own_k = jnp.tile(lax.dynamic_slice_in_dim(k, me * share, share), columns)
    sx, lx = sine_table(bx)
    sz, lz = sine_table(nz)
    sl, _ = sine_table(nl)
    to_global = sz @ np.kron(np.eye(modes), sl)
    rows = [r for d in range(1, modes) for r in (d * nl - 1, d * nl)]
    ends = f32(sz[rows])
    order = parity_order(bx)
    lx, s0, s1 = lx[order], f32(sx[0, order]), f32(sx[-1, order])
    got = jnp.stack([unpack(got[d * columns : (d + 1) * columns], share) for d in range(modes)])
    lanes = got.shape[2]
    vf, vl = got[:, :bx], got[:, bx : 2 * bx]
    a0 = got[:, 2 * bx : 2 * bx + nl].reshape(nz, lanes)
    a1 = got[:, 2 * bx + nl : 2 * bx + 2 * nl].reshape(nz, lanes)
    facts = got[0, 2 * bx + 2 * nl : 2 * bx + 2 * nl + 3].astype(jnp.int32)
    level_ids = jnp.arange(sweeps.shape[0], dtype=jnp.int32)
    allowed = jnp.sum(jnp.where(facts[2][:, None] == level_ids, sweeps, 0), axis=1)
    s = jnp.left_shift(jnp.ones_like(facts[2]), 2 * facts[2]).astype(jnp.float32)

    jump = jnp.stack([t for d in range(1, modes) for t in (vf[d], vl[d - 1])])
    jump = jnp.einsum("rj,riq->ijq", ends, jump, precision=HIGHEST)
    ratio = own_k / s
    whole = f32(lx)[:, None, None] + f32(lz)[None, :, None] + ratio
    lift = jump / whole
    m = f32(to_global)
    face0 = jnp.dot(m, a0, precision=HIGHEST) + jnp.sum(lift * s0[:, None, None], axis=0)
    face1 = jnp.dot(m, a1, precision=HIGHEST) + jnp.sum(lift * s1[:, None, None], axis=0)
    tables = {
        "z": f32(sz.sum(axis=0)),
        "perimeter": float(2 * nz + 2 * bx),
        "cells": float(bx * nz),
        "nz": float(nz),
        "bx": bx,
    }
    mu = f32(lz)[:, None] + ratio[None, :]
    west, east = vcycle(face0, face1, facts, mu, tables, allowed, s, own_k, share)
    total = lift + (s0[:, None, None] * west + s1[:, None, None] * east) / whole
    inner = jnp.einsum("rj,ijq->riq", ends, total, precision=HIGHEST)
    none = jnp.zeros((bx, lanes), jnp.float32)
    mt = f32(to_global.T)
    west = jnp.dot(mt, west, precision=HIGHEST).reshape(modes, nl, lanes)
    east = jnp.dot(mt, east, precision=HIGHEST).reshape(modes, nl, lanes)
    parcels = []
    for d in range(modes):
        below = none if d == 0 else inner[2 * d - 2] + vl[d - 1]
        above = none if d == modes - 1 else inner[2 * d + 1] + vf[d + 1]
        parcels.append(pack(jnp.concatenate([below, above, west[d], east[d]]), columns))
    return jnp.concatenate(parcels)


def body(divergence, neighbours, levels, sweeps):
    _, bx, nl, ny = divergence.shape
    modes = lax.axis_size("mode")
    columns = lax.axis_size("blk")
    share = ny // (modes * columns)
    fourier, weights, shift = fourier_table(ny)
    k = f32(shift)
    inv_s = jnp.right_shift(jnp.full_like(levels, 1 << 20), 2 * levels).astype(jnp.float32)[0]
    inv_s = inv_s * (0.5**20)
    lane = jnp.concatenate([(k * inv_s)[None], jnp.full((7, ny), inv_s)])
    vhat, out = forward(divergence, fourier, lane)
    per_row = 128 // share
    extra = -(2 * bx + 2 * nl + 3) % per_row + 3
    facts = jnp.concatenate([neighbours[0], levels, jnp.zeros((extra - 3,), jnp.int32)])
    facts = jnp.broadcast_to(facts.astype(jnp.float32)[:, None], (extra, ny))
    out = jnp.concatenate([out, facts])
    got = exchange(pack(out, modes * columns), 0)
    back = exchange(middle(got, sweeps, k, bx, nl, modes, columns), 1)
    return inverse(vhat, unpack(back, share), weights[:, None] * fourier, lane, divergence.shape)


def solution(mesh):
    return jax.shard_map(
        body,
        mesh=mesh,
        in_specs=(P("blk", None, "mode", None), P("blk", None), P("blk"), P()),
        out_specs=P("blk", None, "mode", None),
        check_vma=False,
    )
```

profile of v0, /device:TPU:0, one launch (start us, length us, event | category | flops | bytes accessed | tf_op | source)
XLA Modules:
  0.0 129.5 jit_solution(12984003911713396287)
XLA Ops:
  0.7 0.8 dynamic_slice.3
  1.4 0.7 add_convert_fusion
  2.3 0.7 broadcast_multiply_fusion
  3.0 0.7 broadcast_add_fusion
  3.8 0.6 concatenate.50.lane
  4.4 26.3 %forward.1 = (f32[1024,1024]{1,0:T(8,128)}, f32[128,1024]{1,0:T(8,128)}) custom-call(f32[1,32,32,1024]{3,2,1,0:T(8,128)} %x.3, bf16[1024,1024]{1,0:T(8,128)(2,1)} %constant.122.clone.fh, bf16[1024,1024]{1,0:T(8,128)(2,1)} %constant.123.clone.fl, bf16[2,512,512]{2,1,0:T(8,128)(2,1)} %constant.120.clone.kh, bf16[2,512,512]{2,1,0:T(8,128)(2,1)} %constant.121.clone.kl, ...), custom_call_target="tpu_custom_call" | custom-call | tf_op jit(solution)/shard_map/forward/pallas_call | solution.py:247
  30.7 1.1 pad_maximum_fusion.1
  32.2 0.9 copy.158
  33.1 1.4 %reshape.315.src = f32[32,33,128]{2,1,0:T(8,128)} reshape(f32[32,132,32]{2,1,0:T(8,128)S(1)} %copy.158) | data formatting | bytes 1081344 | tf_op jit(solution)/shard_map/reshape | solution.py:106
  34.5 21.7 %exchange_0.1 = f32[32,33,128]{2,1,0:T(8,128)} custom-call(f32[32,33,128]{2,1,0:T(8,128)} %reshape.315.src), custom_call_target="tpu_custom_call" | custom-call | tf_op jit(solution)/shard_map/exchange_0/pallas_call | solution.py:88
  56.3 1.2 fusion.97
  62.0 9.5 %multiply_reduce_fusion.1 = (f32[128,256]{0,1:T(8,128)S(1)}, f32[128,256]{0,1:T(8,128)S(1)}, f32[32,128,256]{1,2,0:T(8,128)}) fusion(f32[32]{0:T(128)S(1)} %copy-done.5, f32[32]{0:T(128)S(1)} %copy-done.6, f32[256]{0:T(256)S(1)} %convert_divide_fusion, f32[32,128]{1,0:T(8,128)S(1)} %broadcast_add_fusion, f32[6,32,256]{2,0,1:T(8,128)S(1)} %stack.6, ...), kind=kOutput, calls=%fused_computation.4 | convolution fusion | flops 81723392 | bytes 4673792 | tf_op jit(solution)/shard_map/rj,riq->ijq/dot_general | solution.py:370
  73.0 0.5 fusion.51
  73.5 0.5 multiply_reduce_fusion.2
  74.0 0.4 fusion.18
  77.3 0.5 convolution_select_fusion.1
  77.8 0.5 convolution_select_fusion
  79.4 6.5 %fusion.1 = f32[6,32,256]{2,0,1:T(8,128)S(1)} fusion(f32[6,128,1]{1,0,2:T(8,128)S(1)} %copy-done.4, f32[32,128,256]{1,2,0:T(8,128)} %get-tuple-element.42, f32[128,256]{0,1:T(8,128)S(1)} %copy.174, f32[128,256]{0,1:T(8,128)S(1)} %copy.173, f32[32]{0:T(128)S(1)} %copy-done.5, f32[32]{0:T(128)S(1)} %copy-done.6, f32[256]{0:T(256)S(1)} %convert_divide_fusion, ...), kind=kOutput, calls=%fused_computation.5 | convolution fusion | flops 81788928 | bytes 4673792 | tf_op jit(solution)/shard_map/rj,ijq->riq/dot_general | solution.py:387
  89.4 0.8 pad_maximum_fusion.2.src
  90.2 18.9 %exchange_1.1 = f32[32,32,128]{2,1,0:T(8,128)} custom-call(f32[32,32,128]{2,1,0:T(8,128)} %pad_maximum_fusion.2.src), custom_call_target="tpu_custom_call" | custom-call | tf_op jit(solution)/shard_map/exchange_1/pallas_call | solution.py:88
  109.1 1.6 %reshape.334 = f32[32,128,32]{2,1,0:T(8,128)S(1)} reshape(f32[32,32,128]{2,1,0:T(8,128)} %exchange_1.1) | data formatting | bytes 1048576 | tf_op jit(solution)/shard_map/reshape | solution.py:111
  110.7 0.6 copy.194
  111.3 1.0 copy.195.rows
  112.3 17.1 %inverse.1 = f32[1,32,32,1024]{3,2,1,0:T(8,128)} custom-call(f32[1024,1024]{1,0:T(8,128)} %get-tuple-element.7.vhat, f32[128,1024]{1,0:T(8,128)} %copy.195.rows, bf16[1024,1024]{1,0:T(8,128)(2,1)} %constant.134.clone.fh, bf16[1024,1024]{1,0:T(8,128)(2,1)} %constant.135.clone.fl, bf16[2,512,512]{2,1,0:T(8,128)(2,1)} %constant.132.clone.kh, ...), custom_call_target="tpu_custom_call" | custom-call | tf_op jit(solution)/shard_map/inverse/pallas_call | solution.py:276
  (100 shorter events, 13.6 us)
Async XLA Ops:
  56.3 3.6 %copy-start.2 = (s32[3]{0:T(128)S(1)}, s32[3]{0:T(128)}, u32[]{:S(2)}) copy-start(s32[3]{0:T(128)} %param.31) | copy-start | bytes 40
  60.1 1.9 %copy-start.4 = (f32[6,128,1]{1,0,2:T(8,128)S(1)}, f32[6,128,1]{1,0,2:T(8,128)}, u32[]{:S(2)}) copy-start(f32[6,128,1]{1,0,2:T(8,128)} %constant.141) | copy-start | bytes 9220
  60.1 1.9 %copy-start.5 = (f32[32]{0:T(128)S(1)}, f32[32]{0:T(128)}, u32[]{:S(2)}) copy-start(f32[32]{0:T(128)} %constant.126.clone) | copy-start | bytes 388
  60.1 1.9 %copy-start.6 = (f32[32]{0:T(128)S(1)}, f32[32]{0:T(128)}, u32[]{:S(2)}) copy-start(f32[32]{0:T(128)} %constant.125.clone) | copy-start | bytes 388
  62.0 9.6 %copy-start.1 = (f32[128,128]{1,0:T(8,128)S(1)}, f32[128,128]{1,0:T(8,128)}, u32[]{:S(2)}) copy-start(f32[128,128]{1,0:T(8,128)} %constant.129.clone) | copy-start | bytes 196612
  62.0 11.0 %copy-start.3 = (f32[128]{0:T(128)S(1)}, f32[128]{0:T(128)}, u32[]{:S(2)}) copy-start(f32[128]{0:T(128)} %constant.128.clone) | copy-start | bytes 1540
  62.0 11.4 %copy-start.7 = (f32[128]{0:T(128)S(1)}, f32[128]{0:T(128)}, u32[]{:S(2)}) copy-start(f32[128]{0:T(128)} %constant.130.clone) | copy-start | bytes 1540
  74.0 4.3 %copy-start = (f32[128,128]{1,0:T(8,128)S(1)}, f32[128,128]{1,0:T(8,128)}, u32[]{:S(2)}) copy-start(f32[128,128]{1,0:T(8,128)} %constant.131.clone) | copy-start | bytes 196612
where the time goes:
time: 130 us; the launch traced here: 129 us
  Pallas kernels  84.1 us (65%)
  matrix products  22.9 us (18%)
  local copies, waits for them, and re-layouts  15.9 us (12%)
  other arithmetic  5.38 us (4%)
    pallas_call x2, Pallas kernels, exchange(): pl.pallas_call(functools.partial(exchange_kernel, columns, n), out_shape=...  40.6 us
    pallas_call x1, Pallas kernels, forward(): pl.pallas_call(functools.partial(forward_kernel, bx, nl, lx, s0), grid=(n...  26.3 us
    pallas_call x1, Pallas kernels, inverse(): pl.pallas_call(functools.partial(inverse_kernel, bx, nl, lx, s0, tile), g...  17.1 us
    dot_general x1, matrix products, middle(): jump = jnp.einsum('rj,riq->ijq', ends, jump, precision=HIGHEST)  9.5 us
    dot_general x1, matrix products, middle(): inner = jnp.einsum('rj,ijq->riq', ends, total, precision=HIGHEST)  6.47 us
    dot_general x15, matrix products, beside(): return jnp.dot(values, hot, precision=HIGHEST)  5.83 us

commit v1 on v0

--- a/solution.py
+++ b/solution.py
@@ -12,8 +12,6 @@
 SWEEPS = 2
 CITERS = 8
 DAMPING = 0.8
-HIGH = lax.Precision.HIGH
-HIGHEST = lax.Precision.HIGHEST
 
 
 def sine_table(extent):
@@ -300,19 +298,52 @@
     return rho * (1.0 - power * power) * scale, power * (1.0 - rho2) * scale
 
 
-def vcycle(first_face, last_face, facts, mu, tables, allowed, stiffness, shift, share):
-    lanes = first_face.shape[1]
-    lane = jnp.arange(lanes, dtype=jnp.int32)
-    slot, within = lane // share, lane % share
-    same = within[:, None] == within[None, :]
-    west_hot = (same & (slot[:, None] == facts[0][None, :])).astype(jnp.float32)
-    east_hot = (same & (slot[:, None] == facts[1][None, :])).astype(jnp.float32)
-    direct, across = face_response(mu, tables["bx"])
-    twice = allowed > 1
-    weight = tables["z"][:, None]
-
-    def beside(hot, values):
-        return jnp.dot(values, hot, precision=HIGHEST)
+def split3(array):
+    high, low = split(array)
+    rest = array - high.astype(jnp.float32) - low.astype(jnp.float32)
+    return high, low, rest.astype(jnp.bfloat16)
+
+
+def moved(values, hot):
+    first, second, third = (
+        jnp.dot(part, hot, preferred_element_type=jnp.float32) for part in split3(values)
+    )
+    return first + (second + third)
+
+
+def middle_kernel(
+    bx, nz, lx, s0, jump, a0, a1, rows, slots, lift_table, end_h, end_l, to_h, to_l, from_h, from_l,
+    lz, zsum, west_out, east_out, inner, lift,
+):
+    half = bx // 2
+    lanes = a0.shape[1]
+    west_slot, east_slot = rows[0:1, :], rows[1:2, :]
+    stiffness, twice = rows[2:3, :], rows[3:4, :] > 0.5
+    shift, ratio = rows[4:5, :], rows[5:6, :]
+    mu = lz[...] + ratio
+    lift_rows = lift_table[...]
+
+    sums = []
+    for part in range(2):
+        total = jnp.zeros((nz, lanes), jnp.float32)
+        for c in range(half):
+            i = part * half + c
+            high, low = split(jump[i])
+            both = jnp.concatenate([high, low, high])
+            value = jnp.dot(lift_rows, both, preferred_element_type=jnp.float32)
+            value = value * inverse_of(mu + lx[i])
+            lift[i] = value
+            total = total + s0[i] * value
+        sums.append(total)
+    first_face = dot3(to_h[...], to_l[...], *split(a0[...])) + sums[0] + sums[1]
+    last_face = dot3(to_h[...], to_l[...], *split(a1[...])) + sums[0] - sums[1]
+
+    west_hot = jnp.where(slots[...] == west_slot, 1.0, 0.0)
+    east_hot = jnp.where(slots[...] == east_slot, 1.0, 0.0)
+    link = (west_hot + east_hot).astype(jnp.bfloat16)
+    west_hot, east_hot = west_hot.astype(jnp.bfloat16), east_hot.astype(jnp.bfloat16)
+    direct, across = face_response(mu, bx)
+    weight = zsum[...]
 
     def sweep(west, east):
         return (
@@ -320,27 +351,36 @@
             last_face + across * west + direct * east,
         )
 
-    used_w, used_e = beside(west_hot, last_face), beside(east_hot, first_face)
+    used_w, used_e = moved(last_face, west_hot), moved(first_face, east_hot)
     second = sweep(used_w, used_e)
     first = jnp.where(twice, second[0], first_face)
     last = jnp.where(twice, second[1], last_face)
-    west, east = beside(west_hot, last), beside(east_hot, first)
+    west, east = moved(last, west_hot), moved(first, east_hot)
     change = west + east - jnp.where(twice, used_w + used_e, 0.0)
-    rhs = jnp.sum(change * weight, axis=0) * stiffness
-    diagonal = stiffness * tables["perimeter"] + tables["cells"] * shift
-    coupling = stiffness * tables["nz"]
-    link = west_hot + east_hot
-    correction = DAMPING * rhs / diagonal
+    rhs = jnp.sum(change * weight, axis=0, keepdims=True) * stiffness
+    diagonal = stiffness * float(2 * nz + 2 * bx) + float(bx * nz) * shift
+    coupling = stiffness * float(nz)
+    spread = jnp.zeros((16, lanes), jnp.float32)
+    rhs, diagonal, coupling = rhs + spread, diagonal + spread, coupling + spread
+    step = DAMPING / diagonal
+    correction = step * rhs
     for _ in range(CITERS - 1):
-        linked = beside(link, correction[None])[0]
-        correction = (
-            correction + DAMPING * (rhs - diagonal * correction + coupling * linked) / diagonal
-        )
-    west = west + beside(west_hot, correction[None]) * weight
-    east = east + beside(east_hot, correction[None]) * weight
+        linked = moved(correction, link)
+        correction = correction + step * (rhs - diagonal * correction + coupling * linked)
+    west = west + moved(correction, west_hot)[0:1] * weight
+    east = east + moved(correction, east_hot)[0:1] * weight
     first, last = sweep(west, east)
-    again_w, again_e = beside(west_hot, last), beside(east_hot, first)
-    return jnp.where(twice, again_w, west), jnp.where(twice, again_e, east)
+    west = jnp.where(twice, moved(last, west_hot), west)
+    east = jnp.where(twice, moved(first, east_hot), east)
+
+    west_out[...] = dot3(from_h[...], from_l[...], *split(west))
+    east_out[...] = dot3(from_h[...], from_l[...], *split(east))
+    for part in range(2):
+        face = west + east if part == 0 else west - east
+        for c in range(half):
+            i = part * half + c
+            total = lift[i] + (s0[i] * face) * inverse_of(mu + lx[i])
+            inner[i] = dot3(end_h[...], end_l[...], *split(total))
 
 
 def middle(got, sweeps, k, bx, nl, modes, columns):
@@ -352,47 +392,59 @@
     sz, lz = sine_table(nz)
     sl, _ = sine_table(nl)
     to_global = sz @ np.kron(np.eye(modes), sl)
-    rows = [r for d in range(1, modes) for r in (d * nl - 1, d * nl)]
-    ends = f32(sz[rows])
+    picks = [r for d in range(1, modes) for r in (d * nl - 1, d * nl)]
     order = parity_order(bx)
-    lx, s0, s1 = lx[order], f32(sx[0, order]), f32(sx[-1, order])
+    ends = np.zeros((-(-len(picks) // 16) * 16, nz))
+    ends[: len(picks)] = sz[picks]
+    end_h, end_l = split_table(ends)
+    to_h, to_l = split_table(to_global)
+    from_h, from_l = split_table(to_global.T)
+    lift_table = jnp.concatenate([end_h.T, end_h.T, end_l.T], axis=1)
     got = jnp.stack([unpack(got[d * columns : (d + 1) * columns], share) for d in range(modes)])
     lanes = got.shape[2]
     vf, vl = got[:, :bx], got[:, bx : 2 * bx]
     a0 = got[:, 2 * bx : 2 * bx + nl].reshape(nz, lanes)
     a1 = got[:, 2 * bx + nl : 2 * bx + 2 * nl].reshape(nz, lanes)
-    facts = got[0, 2 * bx + 2 * nl : 2 * bx + 2 * nl + 3].astype(jnp.int32)
+    facts = got[0, 2 * bx + 2 * nl : 2 * bx + 2 * nl + 3]
+    level = facts[2].astype(jnp.int32)
     level_ids = jnp.arange(sweeps.shape[0], dtype=jnp.int32)
-    allowed = jnp.sum(jnp.where(facts[2][:, None] == level_ids, sweeps, 0), axis=1)
-    s = jnp.left_shift(jnp.ones_like(facts[2]), 2 * facts[2]).astype(jnp.float32)
-
-    jump = jnp.stack([t for d in range(1, modes) for t in (vf[d], vl[d - 1])])
-    jump = jnp.einsum("rj,riq->ijq", ends, jump, precision=HIGHEST)
-    ratio = own_k / s
-    whole = f32(lx)[:, None, None] + f32(lz)[None, :, None] + ratio
-    lift = jump / whole
-    m = f32(to_global)
-    face0 = jnp.dot(m, a0, precision=HIGHEST) + jnp.sum(lift * s0[:, None, None], axis=0)
-    face1 = jnp.dot(m, a1, precision=HIGHEST) + jnp.sum(lift * s1[:, None, None], axis=0)
-    tables = {
-        "z": f32(sz.sum(axis=0)),
-        "perimeter": float(2 * nz + 2 * bx),
-        "cells": float(bx * nz),
-        "nz": float(nz),
-        "bx": bx,
-    }
-    mu = f32(lz)[:, None] + ratio[None, :]
-    west, east = vcycle(face0, face1, facts, mu, tables, allowed, s, own_k, share)
-    total = lift + (s0[:, None, None] * west + s1[:, None, None] * east) / whole
-    inner = jnp.einsum("rj,ijq->riq", ends, total, precision=HIGHEST)
+    allowed = jnp.sum(jnp.where(level[:, None] == level_ids, sweeps, 0), axis=1)
+    s = jnp.left_shift(jnp.ones_like(level), 2 * level).astype(jnp.float32)
+    twice = (allowed > 1).astype(jnp.float32)
+    rows = jnp.stack([facts[0], facts[1], s, twice, own_k, own_k / s, s, s])
+    slot, within = np.arange(lanes) // share, np.arange(lanes) % share
+    slots = f32(np.where(within[:, None] == within[None, :], slot[:, None], -2))
+    jump = [t for d in range(1, modes) for t in (vf[d], vl[d - 1])]
+    jump += [jnp.zeros_like(vf[0])] * (ends.shape[0] - len(picks))
+    jump = jnp.stack(jump, axis=1)
+    west, east, inner = pl.pallas_call(
+        functools.partial(
+            middle_kernel,
+            bx,
+            nz,
+            tuple(float(lx[i]) for i in order),
+            tuple(float(sx[0, i]) for i in order),
+        ),
+        out_shape=[
+            jax.ShapeDtypeStruct((nz, lanes), jnp.float32),
+            jax.ShapeDtypeStruct((nz, lanes), jnp.float32),
+            jax.ShapeDtypeStruct((bx, ends.shape[0], lanes), jnp.float32),
+        ],
+        in_specs=[pl.BlockSpec(memory_space=pltpu.VMEM)] * 14,
+        out_specs=[pl.BlockSpec(memory_space=pltpu.VMEM)] * 3,
+        scratch_shapes=[pltpu.VMEM((bx, nz, lanes), jnp.float32)],
+        compiler_params=pltpu.CompilerParams(vmem_limit_bytes=32 * 1024 * 1024),
+        name="middle",
+    )(
+        jump, a0, a1, rows, slots, lift_table, end_h, end_l, to_h, to_l, from_h, from_l,
+        f32(lz[:, None]), f32(sz.sum(axis=0)[:, None]),
+    )
+    west, east = west.reshape(modes, nl, lanes), east.reshape(modes, nl, lanes)
     none = jnp.zeros((bx, lanes), jnp.float32)
-    mt = f32(to_global.T)
-    west = jnp.dot(mt, west, precision=HIGHEST).reshape(modes, nl, lanes)
-    east = jnp.dot(mt, east, precision=HIGHEST).reshape(modes, nl, lanes)
     parcels = []
     for d in range(modes):
-        below = none if d == 0 else inner[2 * d - 2] + vl[d - 1]
-        above = none if d == modes - 1 else inner[2 * d + 1] + vf[d + 1]
+        below = none if d == 0 else inner[:, 2 * d - 2] + vl[d - 1]
+        above = none if d == modes - 1 else inner[:, 2 * d + 1] + vf[d + 1]
         parcels.append(pack(jnp.concatenate([below, above, west[d], east[d]]), columns))
     return jnp.concatenate(parcels)
 

time: 130 us -> 111 us (0.85)
  matrix products: 22.9 us -> 0 us
  Pallas kernels: 84.1 us -> 89.6 us
    dot_general x21 -> x0, matrix products: 22.9 us -> none  [the longest x1 9.5 us: middle(): jump = jnp.einsum('rj,riq->ijq', ends, jump, precision=HIGHEST)]
    pallas_call x0 -> x1, Pallas kernels: none -> 5.46 us  [middle(): pl.pallas_call(functools.partial(middle_kernel, bx, nz, tuple((float(lx[i...]
where the time goes in v1:
time: 111 us
  Pallas kernels  89.6 us (81%)
  local copies, waits for them, and re-layouts  15.5 us (14%)
  other arithmetic  4.8 us (4%)
  between operations  1.17 us (1%)
    pallas_call x2, Pallas kernels, exchange(): pl.pallas_call(functools.partial(exchange_kernel, columns, n), out_shape=...  40.7 us
    pallas_call x1, Pallas kernels, forward(): pl.pallas_call(functools.partial(forward_kernel, bx, nl, lx, s0), grid=(n...  26.3 us
    pallas_call x1, Pallas kernels, inverse(): pl.pallas_call(functools.partial(inverse_kernel, bx, nl, lx, s0, tile), g...  17.1 us
    pallas_call x1, Pallas kernels, middle(): pl.pallas_call(functools.partial(middle_kernel, bx, nz, tuple((float(lx[i...  5.46 us
    reshape x5, local copies, waits for them, and re-layouts, unpack(): rows = parcels.reshape(blocks, -1, share).transpose(1, 0, 2)  2.31 us

profile of v1, /device:TPU:0, one launch (start us, length us, event | category | flops | bytes accessed | tf_op | source)
XLA Modules:
  0.0 111.0 jit_solution(14293174996717100557)
XLA Ops:
  0.7 0.8 dynamic_slice.3
  1.4 0.7 add_convert_fusion
  2.2 0.7 broadcast_multiply_fusion
  2.9 0.6 concatenate.53.lane
  3.6 26.3 %forward.1 = (f32[1024,1024]{1,0:T(8,128)}, f32[128,1024]{1,0:T(8,128)}) custom-call(f32[1,32,32,1024]{3,2,1,0:T(8,128)} %x.3, bf16[1024,1024]{1,0:T(8,128)(2,1)} %constant.83.clone.fh, bf16[1024,1024]{1,0:T(8,128)(2,1)} %constant.84.clone.fl, bf16[2,512,512]{2,1,0:T(8,128)(2,1)} %constant.81.clone.kh, bf16[2,512,512]{2,1,0:T(8,128)(2,1)} %constant.82.clone.kl, ...), custom_call_target="tpu_custom_call" | custom-call | tf_op jit(solution)/shard_map/forward/pallas_call | solution.py:245
  29.9 1.1 %pad_maximum_fusion.1 = f32[132,1024]{1,0:T(8,128)S(1)} fusion(f32[128,1024]{1,0:T(8,128)} %get-tuple-element.11, f32[132]{0:T(256)S(1)} %pad.26.clone), kind=kLoop, calls=%fused_computation.1 | loop fusion | flops 135168 | bytes 1065488 | tf_op jit(solution)/shard_map/concatenate | solution.py:467
  31.0 0.3 copy.169
  31.4 0.9 copy.170
  32.3 1.4 %reshape.181.src = f32[32,33,128]{2,1,0:T(8,128)} reshape(f32[32,132,32]{2,1,0:T(8,128)S(1)} %copy.170) | data formatting | bytes 1081344 | tf_op jit(solution)/shard_map/reshape | solution.py:104
  33.7 21.7 %exchange_0.1 = f32[32,33,128]{2,1,0:T(8,128)} custom-call(f32[32,33,128]{2,1,0:T(8,128)} %reshape.181.src), custom_call_target="tpu_custom_call" | custom-call | tf_op jit(solution)/shard_map/exchange_0/pallas_call | solution.py:86
  55.5 1.2 %fusion.2 = (f32[8,33,128]{2,1,0:T(8,128)S(1)}, f32[8,33,128]{2,1,0:T(8,128)S(1)}, f32[8,33,128]{2,1,0:T(8,128)S(1)}, f32[8,33,128]{2,1,0:T(8,128)S(1)}) fusion(f32[32,33,128]{2,1,0:T(8,128)} %exchange_0.1), kind=kLoop, calls=%fused_computation.18 | loop fusion | bytes 1081344 | tf_op jit(solution)/shard_map/slice | solution.py:403
  56.8 0.3 copy.178
  57.4 0.3 copy.175
  58.2 0.3 copy.173
  59.5 0.3 copy.171
  60.1 0.3 fusion.1
  60.9 0.4 stack.22.jump
  61.5 5.5 %middle.1 = (f32[128,256]{1,0:T(8,128)S(1)}, f32[128,256]{1,0:T(8,128)S(1)}, f32[32,16,256]{2,1,0:T(8,128)S(1)}) custom-call(f32[32,16,256]{2,1,0:T(8,128)S(1)} %stack.22.jump, f32[128,256]{1,0:T(8,128)S(1)} %bitcast.57, f32[128,256]{1,0:T(8,128)S(1)} %bitcast.56, f32[8,256]{1,0:T(8,128)S(1)} %stack.24.rows, f32[256,256]{1,0:T(8,128)S(1)} %copy-done, ...), custom_call_target="tpu_custom_call" | custom-call | tf_op jit(solution)/shard_map/middle/pallas_call | solution.py:420
  70.9 0.8 pad_maximum_fusion.2.src
  71.7 18.9 %exchange_1.1 = f32[32,32,128]{2,1,0:T(8,128)} custom-call(f32[32,32,128]{2,1,0:T(8,128)} %pad_maximum_fusion.2.src), custom_call_target="tpu_custom_call" | custom-call | tf_op jit(solution)/shard_map/exchange_1/pallas_call | solution.py:86
  90.7 1.6 %reshape.192 = f32[32,128,32]{2,1,0:T(8,128)S(1)} reshape(f32[32,32,128]{2,1,0:T(8,128)} %exchange_1.1) | data formatting | bytes 1048576 | tf_op jit(solution)/shard_map/reshape | solution.py:109
  92.3 0.6 copy.207
  92.8 1.0 copy.208.rows
  93.9 17.1 %inverse.1 = f32[1,32,32,1024]{3,2,1,0:T(8,128)} custom-call(f32[1024,1024]{1,0:T(8,128)} %get-tuple-element.10.vhat, f32[128,1024]{1,0:T(8,128)} %copy.208.rows, bf16[1024,1024]{1,0:T(8,128)(2,1)} %constant.96.clone.fh, bf16[1024,1024]{1,0:T(8,128)(2,1)} %constant.97.clone.fl, bf16[2,512,512]{2,1,0:T(8,128)(2,1)} %constant.94.clone.kh, ...), custom_call_target="tpu_custom_call" | custom-call | tf_op jit(solution)/shard_map/inverse/pallas_call | solution.py:274
  (84 shorter events, 6.5 us)
Async XLA Ops:
  57.2 1.5 %copy-start.10 = (s32[3]{0:T(128)S(1)}, s32[3]{0:T(128)}, u32[]{:S(2)}) copy-start(s32[3]{0:T(128)} %param.31) | copy-start | bytes 40
  60.0 1.4 %copy-start = (f32[256,256]{1,0:T(8,128)S(1)}, f32[256,256]{1,0:T(8,128)}, u32[]{:S(2)}) copy-start(f32[256,256]{1,0:T(8,128)} %constant.91.clone.slots) | copy-start | bytes 786436
  60.0 1.4 %copy-start.1 = (f32[128,1]{1,0:T(8,128)S(1)}, f32[128,1]{1,0:T(8,128)}, u32[]{:S(2)}) copy-start(f32[128,1]{1,0:T(8,128)} %constant.93.clone.zsum) | copy-start | bytes 1540
  60.0 1.4 %copy-start.2 = (f32[128,1]{1,0:T(8,128)S(1)}, f32[128,1]{1,0:T(8,128)}, u32[]{:S(2)}) copy-start(f32[128,1]{1,0:T(8,128)} %constant.92.clone.lz) | copy-start | bytes 1540
  60.0 1.4 %copy-start.3 = (bf16[128,48]{1,0:T(8,128)(2,1)S(1)}, bf16[128,48]{1,0:T(8,128)(2,1)}, u32[]{:S(2)}) copy-start(bf16[128,48]{1,0:T(8,128)(2,1)} %constant.105.lift_table) | copy-start | bytes 36868
  60.1 1.4 %copy-start.4 = (bf16[128,128]{1,0:T(8,128)(2,1)S(1)}, bf16[128,128]{1,0:T(8,128)(2,1)}, u32[]{:S(2)}) copy-start(bf16[128,128]{1,0:T(8,128)(2,1)} %constant.90.clone.from_l) | copy-start | bytes 98308
  60.1 1.4 %copy-start.5 = (bf16[128,128]{1,0:T(8,128)(2,1)S(1)}, bf16[128,128]{1,0:T(8,128)(2,1)}, u32[]{:S(2)}) copy-start(bf16[128,128]{1,0:T(8,128)(2,1)} %constant.89.clone.from_h) | copy-start | bytes 98308
  60.1 1.4 %copy-start.6 = (bf16[128,128]{1,0:T(8,128)(2,1)S(1)}, bf16[128,128]{1,0:T(8,128)(2,1)}, u32[]{:S(2)}) copy-start(bf16[128,128]{1,0:T(8,128)(2,1)} %constant.88.clone.to_l) | copy-start | bytes 98308
  60.1 1.4 %copy-start.7 = (bf16[128,128]{1,0:T(8,128)(2,1)S(1)}, bf16[128,128]{1,0:T(8,128)(2,1)}, u32[]{:S(2)}) copy-start(bf16[128,128]{1,0:T(8,128)(2,1)} %constant.87.clone.to_h) | copy-start | bytes 98308
  60.1 1.4 %copy-start.8 = (bf16[16,128]{1,0:T(8,128)(2,1)S(1)}, bf16[16,128]{1,0:T(8,128)(2,1)}, u32[]{:S(2)}) copy-start(bf16[16,128]{1,0:T(8,128)(2,1)} %constant.86.clone.end_l) | copy-start | bytes 12292
  60.1 1.4 %copy-start.9 = (bf16[16,128]{1,0:T(8,128)(2,1)S(1)}, bf16[16,128]{1,0:T(8,128)(2,1)}, u32[]{:S(2)}) copy-start(bf16[16,128]{1,0:T(8,128)(2,1)} %constant.85.clone.end_h) | copy-start | bytes 12292

commit v2 on v1

--- a/solution.py
+++ b/solution.py
@@ -144,7 +144,8 @@
     return [np.kron(sx[: bx // 2, part::2], sl) for part in (0, 1)]
 
 
-def forward_kernel(bx, nl, lx, s0, x, fh, fl, kh, kl, lam, e0, e1, lane, vhat, rows, ah, al):
+def forward_kernel(bx, nl, lx, s0, x, fh, fl, kh, kl, lam, e0, e1, lane, facts, vhat, *rest):
+    parcels, rows, ah, al = rest if len(rest) == 4 else (None,) + rest
     half = bx // 2
     side = half * nl
 
@@ -177,14 +178,28 @@
         sums.append(total)
     rows[pl.ds(2 * bx, nl), :] = sums[0] + sums[1]
     rows[pl.ds(2 * bx + nl, nl), :] = sums[0] - sums[1]
-
-
-def inverse_kernel(bx, nl, lx, s0, tile, vhat, rows, fh, fl, kh, kl, lam, e0, e1, lane, out, uh, ul):
+    if parcels is not None:
+        for h in range(parcels.shape[0] // 4):
+            here = pl.ds(h * 128, 128)
+            groups = lane_groups([rows[pl.ds(g * bx, bx), here] for g in range(4)])
+            for c in range(4):
+                parcels[h * 4 + c, pl.ds(0, bx), :] = groups[c]
+                parcels[h * 4 + c, pl.ds(bx, 8), :] = facts[...]
+
+
+def inverse_kernel(bx, nl, lx, s0, tile, vhat, got, fh, fl, kh, kl, lam, e0, e1, lane, out, uh, ul, *rest):
+    rows = rest[0] if rest else got
     half = bx // 2
     side = half * nl
 
     @pl.when(pl.program_id(0) == 0)
     def _():
+        if rest:
+            for h in range(got.shape[0] // 4):
+                groups = lane_groups([got[h * 4 + c] for c in range(4)])
+                for g in range(4):
+                    rows[pl.ds(g * bx, bx), pl.ds(h * 128, 128)] = groups[g]
+
         @pl.loop(0, vhat.shape[1] // tile)
         def _(step):
             q = pl.ds(pl.multiple_of(step * tile, tile), tile)
@@ -212,17 +227,33 @@
         out[0, bx - 1 - c] = even[here] - odd[here]
 
 
-def local_tables(bx, nl):
+def local_tables(bx, nl, tile):
     sx, lx = sine_table(bx)
     sl, ll = sine_table(nl)
     order = parity_order(bx)
     return (
         tuple(float(lx[i]) for i in order),
         tuple(float(sx[0, i]) for i in order),
-        f32(ll[:, None]),
-        f32(sl[0][:, None]),
-        f32(sl[-1][:, None]),
+        f32(np.tile(ll[:, None], (1, tile))),
+        f32(np.tile(sl[0][:, None], (1, tile))),
+        f32(np.tile(sl[-1][:, None], (1, tile))),
     )
+
+
+def lane_groups(arrays):
+    count = len(arrays)
+    width = 128 // count
+    group = lax.broadcasted_iota(jnp.int32, arrays[0].shape, 1)
+    results = []
+    for k in range(count):
+        result = arrays[k]
+        for j in range(count):
+            if j != k:
+                turned = pltpu.roll(arrays[j], (j - k) * width % 128, 1)
+                here = (group >= j * width) & (group < (j + 1) * width)
+                result = jnp.where(here, turned, result)
+        results.append(result)
+    return results
 
 
 def whole_block(array):
@@ -232,45 +263,49 @@
 LIMIT = 56 * 1024 * 1024
 
 
-def forward(divergence, fourier, lane):
+def forward(divergence, fourier, lane, facts, blocks):
     _, bx, nl, ny = divergence.shape
     tile = min(256, ny)
-    lx, s0, lam, e0, e1 = local_tables(bx, nl)
+    lx, s0, lam, e0, e1 = local_tables(bx, nl, tile)
     even, odd = parity_tables(bx, nl)
     kh, kl = split_table(np.stack([even.T, odd.T]))
     fh, fl = split_table(fourier.T)
     across = pl.BlockSpec((ny, tile), lambda t: (0, t))
     cells = bx * nl
     count = 2 * bx + 2 * nl
+    rows_shape = jax.ShapeDtypeStruct((count, ny), jnp.float32)
+    rows_spec = pl.BlockSpec((count, tile), lambda t: (0, t))
+    scratch = [pltpu.VMEM((cells, ny), jnp.bfloat16)] * 2
+    if blocks:
+        rows_shape = jax.ShapeDtypeStruct((blocks, bx + 8, 128), jnp.float32)
+        rows_spec = pl.BlockSpec((blocks * tile // ny, bx + 8, 128), lambda t: (t, 0, 0))
+        scratch = [pltpu.VMEM((count, tile), jnp.float32)] + scratch
     return pl.pallas_call(
         functools.partial(forward_kernel, bx, nl, lx, s0),
         grid=(ny // tile,),
-        out_shape=[
-            jax.ShapeDtypeStruct((cells, ny), jnp.float32),
-            jax.ShapeDtypeStruct((count, ny), jnp.float32),
-        ],
+        out_shape=[jax.ShapeDtypeStruct((cells, ny), jnp.float32), rows_shape],
         in_specs=[whole_block(divergence), across, across]
         + [whole_block(a) for a in (kh, kl, lam, e0, e1)]
-        + [pl.BlockSpec((8, tile), lambda t: (0, t))],
-        out_specs=[
-            pl.BlockSpec((cells, tile), lambda t: (0, t)),
-            pl.BlockSpec((count, tile), lambda t: (0, t)),
-        ],
-        scratch_shapes=[pltpu.VMEM((cells, ny), jnp.bfloat16)] * 2,
+        + [pl.BlockSpec((8, tile), lambda t: (0, t)), whole_block(facts)],
+        out_specs=[pl.BlockSpec((cells, tile), lambda t: (0, t)), rows_spec],
+        scratch_shapes=scratch,
         compiler_params=pltpu.CompilerParams(vmem_limit_bytes=LIMIT),
         name="forward",
-    )(divergence, fh, fl, kh, kl, lam, e0, e1, lane)
+    )(divergence, fh, fl, kh, kl, lam, e0, e1, lane, facts)
 
 
 def inverse(vhat, rows, weighted, lane, shape):
     _, bx, nl, ny = shape
     tile = min(256, ny)
-    lx, s0, lam, e0, e1 = local_tables(bx, nl)
+    lx, s0, lam, e0, e1 = local_tables(bx, nl, tile)
     even, odd = parity_tables(bx, nl)
     kh, kl = split_table(np.stack([even, odd]))
     fh, fl = split_table(weighted)
     across = pl.BlockSpec((ny, tile), lambda t: (0, t))
     cells = bx * nl
+    scratch = [pltpu.VMEM((cells, ny), jnp.bfloat16)] * 2
+    if rows.ndim == 3:
+        scratch = scratch + [pltpu.VMEM((2 * bx + 2 * nl, ny), jnp.float32)]
     return pl.pallas_call(
         functools.partial(inverse_kernel, bx, nl, lx, s0, tile),
         grid=(ny // tile,),
@@ -278,7 +313,7 @@
         in_specs=[whole_block(vhat), whole_block(rows), across, across]
         + [whole_block(a) for a in (kh, kl, lam, e0, e1, lane)],
         out_specs=pl.BlockSpec((1, bx, nl, tile), lambda t: (0, 0, 0, t)),
-        scratch_shapes=[pltpu.VMEM((cells, ny), jnp.bfloat16)] * 2,
+        scratch_shapes=scratch,
         compiler_params=pltpu.CompilerParams(vmem_limit_bytes=LIMIT),
         name="inverse",
     )(vhat, rows, fh, fl, kh, kl, lam, e0, e1, lane)
@@ -400,12 +435,20 @@
     to_h, to_l = split_table(to_global)
     from_h, from_l = split_table(to_global.T)
     lift_table = jnp.concatenate([end_h.T, end_h.T, end_l.T], axis=1)
-    got = jnp.stack([unpack(got[d * columns : (d + 1) * columns], share) for d in range(modes)])
+    grouped = 4 * share == 128 and bx == nl
+    if grouped:
+        got = got.reshape(modes, columns, bx + 8, 4, share).transpose(0, 3, 2, 1, 4)
+        got = got.reshape(modes, 4, bx + 8, columns * share)
+        facts = got[0, :3, bx]
+        got = got[:, :, :bx].reshape(modes, 4 * bx, columns * share)
+    else:
+        got = [unpack(got[d * columns : (d + 1) * columns], share) for d in range(modes)]
+        got = jnp.stack(got)
+        facts = got[0, 2 * bx + 2 * nl : 2 * bx + 2 * nl + 3]
     lanes = got.shape[2]
     vf, vl = got[:, :bx], got[:, bx : 2 * bx]
     a0 = got[:, 2 * bx : 2 * bx + nl].reshape(nz, lanes)
     a1 = got[:, 2 * bx + nl : 2 * bx + 2 * nl].reshape(nz, lanes)
-    facts = got[0, 2 * bx + 2 * nl : 2 * bx + 2 * nl + 3]
     level = facts[2].astype(jnp.int32)
     level_ids = jnp.arange(sweeps.shape[0], dtype=jnp.int32)
     allowed = jnp.sum(jnp.where(level[:, None] == level_ids, sweeps, 0), axis=1)
@@ -445,7 +488,11 @@
     for d in range(modes):
         below = none if d == 0 else inner[:, 2 * d - 2] + vl[d - 1]
         above = none if d == modes - 1 else inner[:, 2 * d + 1] + vf[d + 1]
-        parcels.append(pack(jnp.concatenate([below, above, west[d], east[d]]), columns))
+        if grouped:
+            parcel = jnp.stack([below, above, west[d], east[d]]).reshape(4, bx, columns, share)
+            parcels.append(parcel.transpose(2, 1, 0, 3).reshape(columns, bx, 128))
+        else:
+            parcels.append(pack(jnp.concatenate([below, above, west[d], east[d]]), columns))
     return jnp.concatenate(parcels)
 
 
@@ -459,15 +506,22 @@
     inv_s = jnp.right_shift(jnp.full_like(levels, 1 << 20), 2 * levels).astype(jnp.float32)[0]
     inv_s = inv_s * (0.5**20)
     lane = jnp.concatenate([(k * inv_s)[None], jnp.full((7, ny), inv_s)])
-    vhat, out = forward(divergence, fourier, lane)
-    per_row = 128 // share
-    extra = -(2 * bx + 2 * nl + 3) % per_row + 3
-    facts = jnp.concatenate([neighbours[0], levels, jnp.zeros((extra - 3,), jnp.int32)])
-    facts = jnp.broadcast_to(facts.astype(jnp.float32)[:, None], (extra, ny))
-    out = jnp.concatenate([out, facts])
-    got = exchange(pack(out, modes * columns), 0)
+    n = modes * columns
+    facts = jnp.concatenate([neighbours[0], levels]).astype(jnp.float32)
+    table = weights[:, None] * fourier
+    if 4 * share == 128 and bx == nl:
+        tag = jnp.concatenate([jnp.repeat(facts, share), jnp.zeros((share,), jnp.float32)])
+        tag = jnp.broadcast_to(tag[None], (8, 128))
+        vhat, parcels = forward(divergence, fourier, lane, tag, n)
+        back = exchange(middle(exchange(parcels, 0), sweeps, k, bx, nl, modes, columns), 1)
+        return inverse(vhat, back, table, lane, divergence.shape)
+    vhat, out = forward(divergence, fourier, lane, jnp.zeros((8, 128), jnp.float32), 0)
+    extra = -(2 * bx + 2 * nl + 3) % (128 // share) + 3
+    facts = jnp.concatenate([facts, jnp.zeros((extra - 3,), jnp.float32)])
+    out = jnp.concatenate([out, jnp.broadcast_to(facts[:, None], (extra, ny))])
+    got = exchange(pack(out, n), 0)
     back = exchange(middle(got, sweeps, k, bx, nl, modes, columns), 1)
-    return inverse(vhat, unpack(back, share), weights[:, None] * fourier, lane, divergence.shape)
+    return inverse(vhat, unpack(back, share), table, lane, divergence.shape)
 
 
 def solution(mesh):

time: 111 us -> 115 us (1.036)
  Pallas kernels: 89.6 us -> 92.8 us
    another operation x0 -> x29, local copies, waits for them, and re-layouts: none -> 3.13 us  [middle(): jnp.stack([below, above, west[d], east[d]]).reshape(4, bx, columns, share)]
    pallas_call x2, Pallas kernels: 40.7 us -> 43 us  [exchange(): pl.pallas_call(functools.partial(exchange_kernel, columns, n), out_shape=...]
    transpose x3, other arithmetic: 0.62 us -> 2.37 us  [middle(): parcels.append(parcel.transpose(2, 1, 0, 3).reshape(columns, bx, 128))]
    slice x6 -> x2, local copies, waits for them, and re-layouts: 1.63 us -> 0.38 us  [middle(): got = got[:, :, :bx].reshape(modes, 4 * bx, columns * share)]
    reshape x11 -> x7, local copies, waits for them, and re-layouts: 5.4 us -> 6.04 us  [the longest x1 2.43 us: middle(): got = got.reshape(modes, 4, bx + 8, columns * share)]
    transpose x10 -> x1, local copies, waits for them, and re-layouts: 3.53 us -> 3.01 us  [middle(): got = got.reshape(modes, columns, bx + 8, 4, share).transpose(0, 3, 2, 1, 4)]
where the time goes in v2:
time: 115 us
  Pallas kernels  92.8 us (81%)
  local copies, waits for them, and re-layouts  15.4 us (13%)
  other arithmetic  5.37 us (5%)
  between operations  1.21 us (1%)
    pallas_call x2, Pallas kernels, exchange(): pl.pallas_call(functools.partial(exchange_kernel, columns, n), out_shape=...  43 us
    pallas_call x1, Pallas kernels, forward(): pl.pallas_call(functools.partial(forward_kernel, bx, nl, lx, s0), grid=(n...  27 us
    pallas_call x1, Pallas kernels, inverse(): pl.pallas_call(functools.partial(inverse_kernel, bx, nl, lx, s0, tile), g...  17.4 us
    pallas_call x1, Pallas kernels, middle(): pl.pallas_call(functools.partial(middle_kernel, bx, nz, tuple((float(lx[i...  5.45 us
    another operation x29, local copies, waits for them, and re-layouts, middle(): jnp.stack([below, above, west[d], east[d]]).reshape(4, bx, columns, share)  3.13 us
    transpose x1, local copies, waits for them, and re-layouts, middle(): got = got.reshape(modes, columns, bx + 8, 4, share).transpose(0, 3, 2, 1, 4)  3.01 us
    reshape x1, local copies, waits for them, and re-layouts, middle(): got = got.reshape(modes, 4, bx + 8, columns * share)  2.43 us
    transpose x3, other arithmetic, middle(): parcels.append(parcel.transpose(2, 1, 0, 3).reshape(columns, bx, 128))  2.37 us

profile of v2, /device:TPU:0, one launch (start us, length us, event | category | flops | bytes accessed | tf_op | source)
XLA Modules:
  0.0 114.9 jit_solution(10985679045241560151)
XLA Ops:
  0.7 0.7 broadcast_multiply_fusion
  1.4 0.6 concatenate.19.lane
  2.0 0.7 add_convert_fusion
  2.9 0.6 broadcast_in_dim.26.facts
  3.5 27.0 %forward.1 = (f32[1024,1024]{1,0:T(8,128)}, f32[32,40,128]{2,1,0:T(8,128)}) custom-call(f32[1,32,32,1024]{3,2,1,0:T(8,128)} %x.5, bf16[1024,1024]{1,0:T(8,128)(2,1)} %constant.80.clone.fh, bf16[1024,1024]{1,0:T(8,128)(2,1)} %constant.81.clone.fl, bf16[2,512,512]{2,1,0:T(8,128)(2,1)} %constant.78.clone.kh, bf16[2,512,512]{2,1,0:T(8,128)(2,1)} %constant.79.clone.kl, ...), custom_call_target="tpu_custom_call" | custom-call | tf_op jit(solution)/shard_map/forward/pallas_call | solution.py:283
  30.4 23.9 %exchange_0.1 = f32[32,40,128]{2,1,0:T(8,128)} custom-call(f32[32,40,128]{2,1,0:T(8,128)} %get-tuple-element.11.src), custom_call_target="tpu_custom_call" | custom-call | tf_op jit(solution)/shard_map/exchange_0/pallas_call | solution.py:86
  54.4 2.3 %reshape.142 = f32[4,8,40,4,32]{4,3,2,1,0:T(4,128)S(1)} reshape(f32[32,40,128]{2,1,0:T(8,128)} %exchange_0.1) | data formatting | bytes 1310720 | tf_op jit(solution)/shard_map/reshape | solution.py:440
  56.7 3.0 %copy.64 = f32[4,4,40,8,32]{4,3,2,1,0:T(8,128)} copy(f32[4,4,40,8,32]{4,1,2,3,0:T(4,128)S(1)} %bitcast.65) | data formatting | bytes 1310720 | tf_op jit(solution)/shard_map/transpose | solution.py:440
  59.7 2.4 %reshape.143 = f32[4,4,40,256]{3,2,1,0:T(8,128)S(1)} reshape(f32[4,4,40,8,32]{4,3,2,1,0:T(8,128)} %copy.64) | data formatting | bytes 1310720 | tf_op jit(solution)/shard_map/reshape | solution.py:441
  62.3 0.3 copy.65
  62.9 0.4 stack.68.jump
  63.5 0.8 dynamic_slice.3
  64.5 5.5 %middle.1 = (f32[128,256]{1,0:T(8,128)S(1)}, f32[128,256]{1,0:T(8,128)S(1)}, f32[32,16,256]{2,1,0:T(8,128)S(1)}) custom-call(f32[32,16,256]{2,1,0:T(8,128)S(1)} %stack.68.jump, f32[128,256]{1,0:T(8,128)S(1)} %bitcast.63, f32[128,256]{1,0:T(8,128)S(1)} %bitcast.64, f32[8,256]{1,0:T(8,128)S(1)} %stack.69.rows, f32[256,256]{1,0:T(8,128)S(1)} %copy-done, ...), custom_call_target="tpu_custom_call" | custom-call | tf_op jit(solution)/shard_map/middle/pallas_call | solution.py:463
  70.4 0.6 fusion.5
  72.1 1.2 %maximum_bitcast_fusion = (f32[8,32,4,32]{3,2,1,0:T(4,128)S(1)}, f32[8,32,4,32]{3,2,1,0:T(4,128)S(1)}) fusion(f32[1,32,8,32]{3,0,1,2:T(1,128)S(1)} %copy.70, f32[1,32,8,32]{3,0,1,2:T(1,128)S(1)} %copy.69, f32[1,32,8,32]{3,0,1,2:T(1,128)S(1)} %copy.68, f32[1,32,8,32]{3,0,1,2:T(1,128)S(1)} %stack.65, f32[1,32,8,32]{3,0,1,2:T(1,128)S(1)} %copy.81, ...), kind=kLoop, calls=%fused_computation | loop fusion | flops 196608 | bytes 491520 | tf_op jit(solution)/shard_map/transpose | solution.py:493
  73.2 0.3 reshape.150
  74.4 0.6 maximum_bitcast_fusion.2
  75.0 0.3 reshape.149
  76.2 0.6 maximum_bitcast_fusion.1
  76.8 0.3 reshape.148
  77.1 0.5 reshape.147
  77.6 0.8 pad_maximum_fusion.src
  78.4 19.0 %exchange_1.1.got = f32[32,32,128]{2,1,0:T(8,128)} custom-call(f32[32,32,128]{2,1,0:T(8,128)} %pad_maximum_fusion.src), custom_call_target="tpu_custom_call" | custom-call | tf_op jit(solution)/shard_map/exchange_1/pallas_call | solution.py:86
  97.4 17.4 %inverse.1 = f32[1,32,32,1024]{3,2,1,0:T(8,128)} custom-call(f32[1024,1024]{1,0:T(8,128)} %get-tuple-element.10.vhat, f32[32,32,128]{2,1,0:T(8,128)} %exchange_1.1.got, bf16[1024,1024]{1,0:T(8,128)(2,1)} %constant.93.clone.fh, bf16[1024,1024]{1,0:T(8,128)(2,1)} %constant.94.clone.fl, bf16[2,512,512]{2,1,0:T(8,128)(2,1)} %constant.91.clone.kh, ...), custom_call_target="tpu_custom_call" | custom-call | tf_op jit(solution)/shard_map/inverse/pallas_call | solution.py:309
  (70 shorter events, 3.9 us)
Async XLA Ops:
  62.1 1.2 %copy-start.10 = (s32[3]{0:T(128)S(1)}, s32[3]{0:T(128)}, u32[]{:S(2)}) copy-start(s32[3]{0:T(128)} %param.31) | copy-start | bytes 40
  62.1 2.2 %copy-start = (f32[256,256]{1,0:T(8,128)S(1)}, f32[256,256]{1,0:T(8,128)}, u32[]{:S(2)}) copy-start(f32[256,256]{1,0:T(8,128)} %constant.88.clone.slots) | copy-start | bytes 786436
  62.1 2.2 %copy-start.1 = (f32[128,1]{1,0:T(8,128)S(1)}, f32[128,1]{1,0:T(8,128)}, u32[]{:S(2)}) copy-start(f32[128,1]{1,0:T(8,128)} %constant.89.clone.lz) | copy-start | bytes 1540
  62.2 2.2 %copy-start.2 = (f32[128,1]{1,0:T(8,128)S(1)}, f32[128,1]{1,0:T(8,128)}, u32[]{:S(2)}) copy-start(f32[128,1]{1,0:T(8,128)} %constant.90.clone.zsum) | copy-start | bytes 1540
  62.2 2.2 %copy-start.3 = (bf16[128,48]{1,0:T(8,128)(2,1)S(1)}, bf16[128,48]{1,0:T(8,128)(2,1)}, u32[]{:S(2)}) copy-start(bf16[128,48]{1,0:T(8,128)(2,1)} %constant.104.lift_table) | copy-start | bytes 36868
  62.2 2.2 %copy-start.4 = (bf16[128,128]{1,0:T(8,128)(2,1)S(1)}, bf16[128,128]{1,0:T(8,128)(2,1)}, u32[]{:S(2)}) copy-start(bf16[128,128]{1,0:T(8,128)(2,1)} %constant.84.clone.to_h) | copy-start | bytes 98308
  62.2 2.2 %copy-start.5 = (bf16[128,128]{1,0:T(8,128)(2,1)S(1)}, bf16[128,128]{1,0:T(8,128)(2,1)}, u32[]{:S(2)}) copy-start(bf16[128,128]{1,0:T(8,128)(2,1)} %constant.85.clone.to_l) | copy-start | bytes 98308
  62.2 2.2 %copy-start.6 = (bf16[128,128]{1,0:T(8,128)(2,1)S(1)}, bf16[128,128]{1,0:T(8,128)(2,1)}, u32[]{:S(2)}) copy-start(bf16[128,128]{1,0:T(8,128)(2,1)} %constant.86.clone.from_h) | copy-start | bytes 98308
  62.2 2.2 %copy-start.7 = (bf16[128,128]{1,0:T(8,128)(2,1)S(1)}, bf16[128,128]{1,0:T(8,128)(2,1)}, u32[]{:S(2)}) copy-start(bf16[128,128]{1,0:T(8,128)(2,1)} %constant.87.clone.from_l) | copy-start | bytes 98308
  62.2 2.2 %copy-start.8 = (bf16[16,128]{1,0:T(8,128)(2,1)S(1)}, bf16[16,128]{1,0:T(8,128)(2,1)}, u32[]{:S(2)}) copy-start(bf16[16,128]{1,0:T(8,128)(2,1)} %constant.82.clone.end_h) | copy-start | bytes 12292
  62.2 2.2 %copy-start.9 = (bf16[16,128]{1,0:T(8,128)(2,1)S(1)}, bf16[16,128]{1,0:T(8,128)(2,1)}, u32[]{:S(2)}) copy-start(bf16[16,128]{1,0:T(8,128)(2,1)} %constant.83.clone.end_l) | copy-start | bytes 12292

commit v3 on v2

--- a/solution.py
+++ b/solution.py
@@ -418,6 +418,58 @@
             inner[i] = dot3(end_h[...], end_l[...], *split(total))
 
 
+def grouped_kernel(
+    bx, nl, modes, columns, levels, lx, s0, sweeps, got, own_k, slots, lift_table, end_h, end_l, to_h, to_l,
+    from_h, from_l, lz, zsum, parcels, lift, parts, rows, jump, inner, a0, a1, west, east,
+):
+    nz = nl * modes
+    for d in range(modes):
+        for h in range(columns // 4):
+            here = pl.ds(h * 128, 128)
+            groups = lane_groups([got[d * columns + h * 4 + c] for c in range(4)])
+            for g in range(2):
+                parts[d, g, :, here] = groups[g][:bx]
+            a0[pl.ds(d * nl, nl), here] = groups[2][:nl]
+            a1[pl.ds(d * nl, nl), here] = groups[3][:nl]
+            if d == 0:
+                for g in range(3):
+                    rows[pl.ds(g, 1), here] = groups[g][bx : bx + 1]
+    level = rows[2:3, :]
+    stiffness = jnp.zeros_like(level)
+    allowed = jnp.zeros_like(level)
+    for number in range(levels):
+        stiffness = jnp.where(level == float(number), float(4**number), stiffness)
+        allowed = jnp.where(level == float(number), sweeps[number].astype(jnp.float32), allowed)
+    rows[2:3, :] = stiffness
+    rows[3:4, :] = jnp.where(allowed > 1.5, 1.0, 0.0)
+    rows[4:5, :] = own_k[0:1, :]
+    rows[5:6, :] = own_k[0:1, :] / stiffness
+    jump[...] = jnp.zeros(jump.shape, jnp.float32)
+    for d in range(1, modes):
+        for i in range(bx):
+            jump[i, pl.ds(2 * d - 2, 1), :] = parts[d, 0, pl.ds(i, 1), :]
+            jump[i, pl.ds(2 * d - 1, 1), :] = parts[d - 1, 1, pl.ds(i, 1), :]
+    middle_kernel(
+        bx, nz, lx, s0, jump, a0, a1, rows, slots, lift_table, end_h, end_l, to_h, to_l, from_h, from_l,
+        lz, zsum, west, east, inner, lift,
+    )
+    for d in range(1, modes):
+        for i in range(bx):
+            one = pl.ds(i, 1)
+            parts[d - 1, 1, one, :] = parts[d - 1, 1, one, :] + inner[i, pl.ds(2 * d - 2, 1), :]
+            parts[d, 0, one, :] = parts[d, 0, one, :] + inner[i, pl.ds(2 * d - 1, 1), :]
+    none = jnp.zeros((bx, 128), jnp.float32)
+    for d in range(modes):
+        for h in range(columns // 4):
+            here = pl.ds(h * 128, 128)
+            below = parts[d - 1, 1, :, here] if d > 0 else none
+            above = parts[d + 1, 0, :, here] if d < modes - 1 else none
+            slab = pl.ds(d * nl, nl)
+            groups = lane_groups([below, above, west[slab, here], east[slab, here]])
+            for c in range(4):
+                parcels[d * columns + h * 4 + c] = groups[c]
+
+
 def middle(got, sweeps, k, bx, nl, modes, columns):
     nz = nl * modes
     share = k.shape[0] // (modes * columns)
@@ -435,16 +487,36 @@
     to_h, to_l = split_table(to_global)
     from_h, from_l = split_table(to_global.T)
     lift_table = jnp.concatenate([end_h.T, end_h.T, end_l.T], axis=1)
-    grouped = 4 * share == 128 and bx == nl
+    slot, within = np.arange(columns * share) // share, np.arange(columns * share) % share
+    slots = f32(np.where(within[:, None] == within[None, :], slot[:, None], -2))
+    numbers = (tuple(float(lx[i]) for i in order), tuple(float(sx[0, i]) for i in order))
+    tables = (
+        slots, lift_table, end_h, end_l, to_h, to_l, from_h, from_l,
+        f32(lz[:, None]), f32(sz.sum(axis=0)[:, None]),
+    )
+    grouped = 4 * share == 128 and bx == nl and columns % 4 == 0
     if grouped:
-        got = got.reshape(modes, columns, bx + 8, 4, share).transpose(0, 3, 2, 1, 4)
-        got = got.reshape(modes, 4, bx + 8, columns * share)
-        facts = got[0, :3, bx]
-        got = got[:, :, :bx].reshape(modes, 4 * bx, columns * share)
-    else:
-        got = [unpack(got[d * columns : (d + 1) * columns], share) for d in range(modes)]
-        got = jnp.stack(got)
-        facts = got[0, 2 * bx + 2 * nl : 2 * bx + 2 * nl + 3]
+        lanes = columns * share
+        own_k = jnp.broadcast_to(own_k[None], (8, lanes))
+        shapes = [
+            (bx, nz, lanes), (modes, 2, bx, lanes), (8, lanes), (bx, ends.shape[0], lanes),
+            (bx, ends.shape[0], lanes), (nz, lanes), (nz, lanes), (nz, lanes), (nz, lanes),
+        ]
+        return pl.pallas_call(
+            functools.partial(
+                grouped_kernel, bx, nl, modes, columns, sweeps.shape[0], numbers[0], numbers[1]
+            ),
+            out_shape=jax.ShapeDtypeStruct((modes * columns, bx, 128), jnp.float32),
+            in_specs=[pl.BlockSpec(memory_space=pltpu.SMEM)]
+            + [pl.BlockSpec(memory_space=pltpu.VMEM)] * (2 + len(tables)),
+            out_specs=pl.BlockSpec(memory_space=pltpu.VMEM),
+            scratch_shapes=[pltpu.VMEM(shape, jnp.float32) for shape in shapes],
+            compiler_params=pltpu.CompilerParams(vmem_limit_bytes=32 * 1024 * 1024),
+            name="middle",
+        )(sweeps, got, own_k, *tables)
+    got = [unpack(got[d * columns : (d + 1) * columns], share) for d in range(modes)]
+    got = jnp.stack(got)
+    facts = got[0, 2 * bx + 2 * nl : 2 * bx + 2 * nl + 3]
     lanes = got.shape[2]
     vf, vl = got[:, :bx], got[:, bx : 2 * bx]
     a0 = got[:, 2 * bx : 2 * bx + nl].reshape(nz, lanes)
@@ -488,11 +560,7 @@
     for d in range(modes):
         below = none if d == 0 else inner[:, 2 * d - 2] + vl[d - 1]
         above = none if d == modes - 1 else inner[:, 2 * d + 1] + vf[d + 1]
-        if grouped:
-            parcel = jnp.stack([below, above, west[d], east[d]]).reshape(4, bx, columns, share)
-            parcels.append(parcel.transpose(2, 1, 0, 3).reshape(columns, bx, 128))
-        else:
-            parcels.append(pack(jnp.concatenate([below, above, west[d], east[d]]), columns))
+        parcels.append(pack(jnp.concatenate([below, above, west[d], east[d]]), columns))
     return jnp.concatenate(parcels)
 
 
@@ -509,7 +577,7 @@
     n = modes * columns
     facts = jnp.concatenate([neighbours[0], levels]).astype(jnp.float32)
     table = weights[:, None] * fourier
-    if 4 * share == 128 and bx == nl:
+    if 4 * share == 128 and bx == nl and columns % 4 == 0:
         tag = jnp.concatenate([jnp.repeat(facts, share), jnp.zeros((share,), jnp.float32)])
         tag = jnp.broadcast_to(tag[None], (8, 128))
         vhat, parcels = forward(divergence, fourier, lane, tag, n)

time: 115 us -> 101 us (0.88)
  local copies, waits for them, and re-layouts: 15.4 us -> 4.15 us
  other arithmetic: 5.37 us -> 1.42 us
  Pallas kernels: 92.8 us -> 94.2 us
    reshape x6 -> x0, local copies, waits for them, and re-layouts: 5.95 us -> none  [the longest x1 2.43 us: middle(): got = got.reshape(modes, 4, bx + 8, columns * share)]
    another operation x35 -> x0, local copies, waits for them, and re-layouts: 3.78 us -> none  [the longest x29 3.13 us: middle(): jnp.stack([below, above, west[d], east[d]]).reshape(4, bx, columns, share)]
    transpose x1 -> x0, local copies, waits for them, and re-layouts: 3.01 us -> none  [middle(): got = got.reshape(modes, columns, bx + 8, 4, share).transpose(0, 3, 2, 1, 4)]
    transpose x3 -> x0, other arithmetic: 2.37 us -> none  [middle(): parcels.append(parcel.transpose(2, 1, 0, 3).reshape(columns, bx, 128))]
    unnamed x22 -> x26, local copies, waits for them, and re-layouts: 0.07 us -> 1.93 us
    pallas_call x1, Pallas kernels: 5.45 us -> 6.79 us  [middle(): pl.pallas_call(functools.partial(grouped_kernel, bx, nl, modes, columns,...]
where the time goes in v3:
time: 101 us
  Pallas kernels  94.2 us (93%)
  local copies, waits for them, and re-layouts  4.15 us (4%)
  other arithmetic  1.42 us (1%)
    pallas_call x2, Pallas kernels, exchange(): pl.pallas_call(functools.partial(exchange_kernel, columns, n), out_shape=...  42.9 us
    pallas_call x1, Pallas kernels, forward(): pl.pallas_call(functools.partial(forward_kernel, bx, nl, lx, s0), grid=(n...  27 us
    pallas_call x1, Pallas kernels, inverse(): pl.pallas_call(functools.partial(inverse_kernel, bx, nl, lx, s0, tile), g...  17.4 us
    pallas_call x1, Pallas kernels, middle(): pl.pallas_call(functools.partial(grouped_kernel, bx, nl, modes, columns,...  6.79 us

profile of v3, /device:TPU:0, one launch (start us, length us, event | category | flops | bytes accessed | tf_op | source)
XLA Modules:
  0.0 100.6 jit_solution(11942041335855609268)
XLA Ops:
  0.7 0.8 dynamic_slice.3
  1.4 0.7 add_convert_fusion
  2.2 0.1 broadcast_in_dim.22
  2.2 0.1 reshape.8
  2.3 0.6 broadcast_in_dim.23.facts
  2.9 0.1 broadcast_in_dim.24
  3.0 0.7 broadcast_multiply_fusion
  3.7 0.6 concatenate.12.lane
  4.3 0.0 copy-start.6
  4.3 0.0 copy-start.7
  4.3 0.0 copy-start.8
  4.4 0.0 copy-start.9
  4.4 0.0 copy-start.10
  4.4 0.0 copy-start.11
  4.4 0.0 copy-start.12
  4.4 27.0 %forward.1 = (f32[1024,1024]{1,0:T(8,128)}, f32[32,40,128]{2,1,0:T(8,128)}) custom-call(f32[1,32,32,1024]{3,2,1,0:T(8,128)} %x.5, bf16[1024,1024]{1,0:T(8,128)(2,1)} %constant.73.clone.fh, bf16[1024,1024]{1,0:T(8,128)(2,1)} %constant.74.clone.fl, bf16[2,512,512]{2,1,0:T(8,128)(2,1)} %constant.71.clone.kh, bf16[2,512,512]{2,1,0:T(8,128)(2,1)} %constant.72.clone.kl, ...), custom_call_target="tpu_custom_call" | custom-call | tf_op jit(solution)/shard_map/forward/pallas_call | solution.py:283
  31.4 23.9 %exchange_0.1.got = f32[32,40,128]{2,1,0:T(8,128)} custom-call(f32[32,40,128]{2,1,0:T(8,128)} %get-tuple-element.8.src), custom_call_target="tpu_custom_call" | custom-call | tf_op jit(solution)/shard_map/exchange_0/pallas_call | solution.py:86
  55.4 0.0 copy-done.2
  55.5 1.1 %copy-done = f32[32,40,128]{2,1,0:T(8,128)S(1)} copy-done((f32[32,40,128]{2,1,0:T(8,128)S(1)}, f32[32,40,128]{2,1,0:T(8,128)}, u32[]{:S(2)}) %copy-start) | copy-done | bytes 655384
  56.6 6.8 %middle.1.src = f32[32,32,128]{2,1,0:T(8,128)S(1)} custom-call(s32[3]{0:T(128)S(1)} %copy-done.12, f32[32,40,128]{2,1,0:T(8,128)S(1)} %copy-done, f32[8,256]{1,0:T(8,128)S(1)} %broadcast_in_dim.25.own_k, f32[256,256]{1,0:T(8,128)S(1)} %copy-done.2, bf16[128,48]{1,0:T(8,128)(2,1)S(1)} %copy-done.5, bf16[16,128]{1,0:T(8,128)(2,1)S(1)} %copy-done.11, ...), custom_call_target="tpu_custom_call" | custom-call | tf_op jit(solution)/shard_map/middle/pallas_call | solution.py:505
  63.4 0.0 copy-start.1
  63.4 0.8 copy-done.1
  64.2 19.0 %exchange_1.1.got = f32[32,32,128]{2,1,0:T(8,128)} custom-call(f32[32,32,128]{2,1,0:T(8,128)} %copy-done.1), custom_call_target="tpu_custom_call" | custom-call | tf_op jit(solution)/shard_map/exchange_1/pallas_call | solution.py:86
  83.2 17.4 %inverse.1 = f32[1,32,32,1024]{3,2,1,0:T(8,128)} custom-call(f32[1024,1024]{1,0:T(8,128)} %get-tuple-element.7.vhat, f32[32,32,128]{2,1,0:T(8,128)} %exchange_1.1.got, bf16[1024,1024]{1,0:T(8,128)(2,1)} %constant.86.clone.fh, bf16[1024,1024]{1,0:T(8,128)(2,1)} %constant.87.clone.fl, bf16[2,512,512]{2,1,0:T(8,128)(2,1)} %constant.84.clone.kh, ...), custom_call_target="tpu_custom_call" | custom-call | tf_op jit(solution)/shard_map/inverse/pallas_call | solution.py:309
  (18 shorter events, 0.0 us)
Async XLA Ops:
  4.3 51.1 %copy-start.2 = (f32[256,256]{1,0:T(8,128)S(1)}, f32[256,256]{1,0:T(8,128)}, u32[]{:S(2)}) copy-start(f32[256,256]{1,0:T(8,128)} %constant.81.clone.slots) | copy-start | bytes 786436
  4.3 51.1 %copy-start.3 = (f32[128,1]{1,0:T(8,128)S(1)}, f32[128,1]{1,0:T(8,128)}, u32[]{:S(2)}) copy-start(f32[128,1]{1,0:T(8,128)} %constant.83.clone.zsum) | copy-start | bytes 1540
  4.3 51.1 %copy-start.4 = (f32[128,1]{1,0:T(8,128)S(1)}, f32[128,1]{1,0:T(8,128)}, u32[]{:S(2)}) copy-start(f32[128,1]{1,0:T(8,128)} %constant.82.clone.lz) | copy-start | bytes 1540
  4.3 51.1 %copy-start.5 = (bf16[128,48]{1,0:T(8,128)(2,1)S(1)}, bf16[128,48]{1,0:T(8,128)(2,1)}, u32[]{:S(2)}) copy-start(bf16[128,48]{1,0:T(8,128)(2,1)} %constant.97.lift_table) | copy-start | bytes 36868
  4.3 51.1 %copy-start.6 = (bf16[128,128]{1,0:T(8,128)(2,1)S(1)}, bf16[128,128]{1,0:T(8,128)(2,1)}, u32[]{:S(2)}) copy-start(bf16[128,128]{1,0:T(8,128)(2,1)} %constant.80.clone.from_l) | copy-start | bytes 98308
  4.3 51.1 %copy-start.7 = (bf16[128,128]{1,0:T(8,128)(2,1)S(1)}, bf16[128,128]{1,0:T(8,128)(2,1)}, u32[]{:S(2)}) copy-start(bf16[128,128]{1,0:T(8,128)(2,1)} %constant.79.clone.from_h) | copy-start | bytes 98308
  4.3 51.1 %copy-start.8 = (bf16[128,128]{1,0:T(8,128)(2,1)S(1)}, bf16[128,128]{1,0:T(8,128)(2,1)}, u32[]{:S(2)}) copy-start(bf16[128,128]{1,0:T(8,128)(2,1)} %constant.78.clone.to_l) | copy-start | bytes 98308
  4.4 51.1 %copy-start.9 = (bf16[128,128]{1,0:T(8,128)(2,1)S(1)}, bf16[128,128]{1,0:T(8,128)(2,1)}, u32[]{:S(2)}) copy-start(bf16[128,128]{1,0:T(8,128)(2,1)} %constant.77.clone.to_h) | copy-start | bytes 98308
  4.4 51.1 %copy-start.10 = (bf16[16,128]{1,0:T(8,128)(2,1)S(1)}, bf16[16,128]{1,0:T(8,128)(2,1)}, u32[]{:S(2)}) copy-start(bf16[16,128]{1,0:T(8,128)(2,1)} %constant.76.clone.end_l) | copy-start | bytes 12292
  4.4 51.1 %copy-start.11 = (bf16[16,128]{1,0:T(8,128)(2,1)S(1)}, bf16[16,128]{1,0:T(8,128)(2,1)}, u32[]{:S(2)}) copy-start(bf16[16,128]{1,0:T(8,128)(2,1)} %constant.75.clone.end_h) | copy-start | bytes 12292
  4.4 51.1 %copy-start.12 = (s32[3]{0:T(128)S(1)}, s32[3]{0:T(128)}, u32[]{:S(2)}) copy-start(s32[3]{0:T(128)} %sweeps.1) | copy-start | bytes 40
  55.5 1.1 %copy-start = (f32[32,40,128]{2,1,0:T(8,128)S(1)}, f32[32,40,128]{2,1,0:T(8,128)}, u32[]{:S(2)}) copy-start(f32[32,40,128]{2,1,0:T(8,128)} %exchange_0.1.got) | copy-start | bytes 1966084
  63.4 0.8 copy-start.1
